TPU v7x, 128 devices: a whole 4x4x4 slice. The times are simulated.
128 devices in a mesh: gx: 8 (over y, x_lo), gy: 8 (over x_hi, z), ga: 2 (over core).
Axes of the slice: x: 4 (x_hi: 2, x_lo: 2; x = x_hi * 2 + x_lo), y: 4, z: 4, core: 2. Of those that a mesh axis runs over, the one named last changes fastest.
Arguments:
- fields: float32 [5, 16, 128, 2048], P(None, 'ga', 'gx', 'gy'), may hold values from -6 to 6
- stiffness: float32 [16, 128, 2048], P('ga', 'gx', 'gy'), may hold values from 0.25 to 4
- lift_weight: float32 [5, 32], replicated, may hold values from -2.5 to 2.5
- lift_bias: float32 [32], replicated, may hold values from -3 to 3
- mix_weight: bfloat16 [32, 32], replicated, may hold values from -0.5 to 0.5
- spectral_weight: float32 [8, 32, 32, 32, 128], P('ga', 'gy', None, 'gx'), may hold values from -0.48 to 0.48
- output_bias: float32 [32], replicated, may hold values from -3 to 3
Outputs:
- layer_out: bfloat16 [16, 32, 64, 1024], P('ga', None, 'gx', 'gy')
All inputs are finite; a program needn't handle non-finite values.
Results may differ from a plain program's by a relative error of at most 0.01.
Values may be sent and summed in bfloat16 or wider, within the bound.
No kernel may reach another device: no remote copies, remote signals or barrier semaphores. Data moves between devices by JAX's collectives and lax.ppermute only.
A program may use at most 128 MiB of HBM per device.

v0:
```python
import math
import jax
import jax.numpy as jnp
from jax import lax
from jax.sharding import PartitionSpec as P

STEPS = 3
MX = 32
MY = 64
MZ = 8
courant_half = 0.1
smooth_half = 0.15
mean_flow = (0.3, -0.2, 0.1)
highest = lax.Precision.HIGHEST


def padded_2(block, sides, width):
    for axis, dim in sides:
        count = lax.axis_size(axis)
        forward = [(i, i + 1) for i in range(count - 1)]
        forward.append((count - 1, 0))
        backward = [(target, source) for source, target in forward]
        low = lax.ppermute(
            lax.slice_in_dim(block, block.shape[dim] - width, None, axis=dim), axis, forward
        )
        high = lax.ppermute(lax.slice_in_dim(block, 0, width, axis=dim), axis, backward)
        block = jnp.concatenate([low, block, high], axis=dim)
    return block


def step_interior(padded, stiff_part):
    center = padded[:, 1:-1, 1:-1, 1:-1]
    upper_depth = padded[:, 2:, 1:-1, 1:-1]
    lower_depth = padded[:, :-2, 1:-1, 1:-1]
    upper_east = padded[:, 1:-1, 2:, 1:-1]
    lower_east = padded[:, 1:-1, :-2, 1:-1]
    upper_north = padded[:, 1:-1, 1:-1, 2:]
    lower_north = padded[:, 1:-1, 1:-1, :-2]
    slope_depth = upper_depth - lower_depth
    slope_east = upper_east - lower_east
    slope_north = upper_north - lower_north
    curvature = (
        upper_depth
        + lower_depth
        + upper_east
        + lower_east
        + upper_north
        + lower_north
        - 6.0 * center
    )
    transport = mean_flow[0] * slope_east + mean_flow[1] * slope_north + mean_flow[2] * slope_depth
    diverge = slope_east[1] + slope_north[2] + slope_depth[3]
    coupling = jnp.stack(
        [diverge, slope_east[4], slope_north[4], slope_depth[4], stiff_part * diverge]
    )
    return center - courant_half * (transport + coupling) + smooth_half * curvature


def coarsen(fields_now):
    extent = fields_now.shape
    blocks = fields_now.reshape(extent[0], extent[1], extent[2] // 2, 2, extent[3] // 2, 2)
    return 0.25 * (
        blocks[:, :, :, 0, :, 0]
        + blocks[:, :, :, 1, :, 0]
        + blocks[:, :, :, 0, :, 1]
        + blocks[:, :, :, 1, :, 1]
    )


def angles(frequencies, points, length):
    product = jnp.mod(frequencies[:, None] * points[None, :], length)
    return product.astype(jnp.float32) * (2.0 * math.pi / length)


def centered(number):
    return jnp.arange(number, dtype=jnp.int32) - number // 2


def forward_east_table(points, length, mode_count):
    phases = angles(centered(mode_count), points, length)
    factor = 1.0 / math.sqrt(length)
    return (jnp.stack([jnp.cos(phases).T, -jnp.sin(phases).T], axis=1) * factor).astype(
        jnp.bfloat16
    )


def forward_north_table(points, length, mode_count):
    phases = angles(centered(mode_count), points, length)
    factor = 1.0 / math.sqrt(length)
    cosines = jnp.cos(phases).T * factor
    sines = jnp.sin(phases).T * factor
    return jnp.stack(
        [jnp.concatenate([cosines, -sines], axis=1), jnp.concatenate([sines, cosines], axis=1)],
        axis=0,
    )


def inverse_north_table(points, length, mode_count):
    phases = angles(centered(mode_count), points, length)
    factor = 1.0 / math.sqrt(length)
    cosines = jnp.cos(phases) * factor
    sines = jnp.sin(phases) * factor
    return jnp.concatenate(
        [jnp.stack([cosines, sines], axis=1), jnp.stack([-sines, cosines], axis=1)], axis=0
    )


def inverse_east_table(points, length, mode_count):
    phases = angles(centered(mode_count), points, length)
    factor = 1.0 / math.sqrt(length)
    return jnp.stack([jnp.cos(phases) * factor, -jnp.sin(phases) * factor], axis=1)


def forward_depth_blocks(values, points, frequencies, length):
    slot_count = frequencies.shape[0]
    phases = angles(frequencies.reshape(-1), points, length).reshape(
        slot_count, frequencies.shape[1], points.shape[0]
    )
    factor = 1.0 / math.sqrt(length)
    cosines = jnp.cos(phases) * factor
    sines = jnp.sin(phases) * factor
    halfway = values.shape[-1] // 2
    real_in = values[..., :halfway]
    imag_in = values[..., halfway:]
    real_part = jnp.einsum("zcrbn,rkz->rkcbn", real_in, cosines, precision=highest) + jnp.einsum(
        "zcrbn,rkz->rkcbn", imag_in, sines, precision=highest
    )
    imag_part = jnp.einsum("zcrbn,rkz->rkcbn", imag_in, cosines, precision=highest) - jnp.einsum(
        "zcrbn,rkz->rkcbn", real_in, sines, precision=highest
    )
    return jnp.concatenate([real_part, imag_part], axis=-1)


def mix_channels(coeffs, weight):
    halfway = coeffs.shape[-1] // 2
    real_in = coeffs[..., :halfway]
    imag_in = coeffs[..., halfway:]
    weight_real = weight[..., :halfway]
    weight_imag = weight[..., halfway:]
    real_part = jnp.einsum(
        "kcmn,kmcon->komn", real_in, weight_real, precision=highest
    ) - jnp.einsum("kcmn,kmcon->komn", imag_in, weight_imag, precision=highest)
    imag_part = jnp.einsum(
        "kcmn,kmcon->komn", imag_in, weight_real, precision=highest
    ) + jnp.einsum("kcmn,kmcon->komn", real_in, weight_imag, precision=highest)
    return jnp.concatenate([real_part, imag_part], axis=-1)


def inverse_depth(values, frequencies, points, length):
    phases = angles(frequencies, points, length)
    factor = 1.0 / math.sqrt(length)
    cosines = jnp.cos(phases) * factor
    sines = jnp.sin(phases) * factor
    halfway = values.shape[-1] // 2
    real_in = values[..., :halfway]
    imag_in = values[..., halfway:]
    real_part = jnp.einsum("komn,kz->zomn", real_in, cosines, precision=highest) - jnp.einsum(
        "komn,kz->zomn", imag_in, sines, precision=highest
    )
    imag_part = jnp.einsum("komn,kz->zomn", imag_in, cosines, precision=highest) + jnp.einsum(
        "komn,kz->zomn", real_in, sines, precision=highest
    )
    return jnp.concatenate([real_part, imag_part], axis=-1)


def shards(fields, stiffness, lift_weight, lift_bias, mix_weight, spectral_weight, output_bias):
    east_tiles = lax.axis_size("gx")
    north_tiles = lax.axis_size("gy")
    depth_groups = lax.axis_size("ga")
    fields_now = fields
    for repeat in range(STEPS):
        padded = padded_2(fields_now, (("gx", 2), ("gy", 3), ("ga", 1)), 1)
        fields_now = step_interior(padded, stiffness)
    filtered = coarsen(fields_now)
    pre_lift = (
        jnp.einsum("fzxy,fc->zcxy", filtered, lift_weight, precision=highest)
        + lift_bias[None, :, None, None]
    )
    lifted = jax.nn.gelu(pre_lift, approximate=True).astype(jnp.bfloat16)
    depth_local = lifted.shape[0]
    length_east = lifted.shape[2] * east_tiles
    length_north = lifted.shape[3] * north_tiles
    length_depth = depth_local * depth_groups
    east_points = jnp.arange(length_east, dtype=jnp.int32)
    north_points = jnp.arange(length_north, dtype=jnp.int32)
    table_east = forward_east_table(east_points, length_east, MX)
    table_north = forward_north_table(north_points, length_north, MY)
    planes = lax.all_to_all(
        lax.all_to_all(lifted, "gx", split_axis=1, concat_axis=2, tiled=True),
        "gy",
        split_axis=0,
        concat_axis=3,
        tiled=True,
    )
    east_modes = jnp.einsum(
        "zcxy,xpm->zcpmy", planes, table_east, preferred_element_type=jnp.float32
    )
    north_modes = jnp.einsum("zcpmy,pyq->zcmq", east_modes, table_north, precision=highest)
    plane_count = planes.shape[0]
    depth_points = (
        lax.axis_index("ga") * depth_local
        + lax.axis_index("gy") * plane_count
        + jnp.arange(plane_count, dtype=jnp.int32)
    )
    block_east = MX // north_tiles
    block_depth = MZ // depth_groups
    grouped = north_modes.reshape(
        plane_count, north_modes.shape[1], north_tiles, block_east, 2 * MY
    )
    owners = jnp.arange(1 * lax.axis_size(("gy", "ga")), dtype=jnp.int32)
    picked = jnp.take(grouped, owners // depth_groups, axis=2)
    frequencies = (owners % depth_groups)[:, None] * block_depth + jnp.arange(
        block_depth, dtype=jnp.int32
    )[None, :]
    coeffs = lax.psum_scatter(
        forward_depth_blocks(picked, depth_points, frequencies, length_depth).astype(jnp.bfloat16),
        ("gy", "ga"),
        scatter_dimension=0,
        tiled=True,
    ).astype(jnp.float32)[0]
    mixed_modes = mix_channels(lax.all_gather(coeffs, "gx", axis=1, tiled=True), spectral_weight)
    own_frequencies = lax.axis_index("ga") * coeffs.shape[0] + jnp.arange(
        coeffs.shape[0], dtype=jnp.int32
    )
    points = jnp.arange(depth_local * lax.axis_size("ga"), dtype=jnp.int32)
    back_depth = lax.psum_scatter(
        inverse_depth(mixed_modes, own_frequencies, points, length_depth),
        "ga",
        scatter_dimension=0,
        tiled=True,
    )
    back_north = jnp.einsum(
        "zomq,qpy->zompy",
        back_depth,
        inverse_north_table(north_points, length_north, MY),
        precision=highest,
    )
    all_modes = lax.all_to_all(back_north, "gy", split_axis=4, concat_axis=2, tiled=True)
    spectral = jnp.einsum(
        "zompy,mpx->zoxy",
        all_modes,
        inverse_east_table(east_points, length_east, MX),
        precision=highest,
    ).astype(jnp.bfloat16)
    spectral = lax.all_to_all(spectral, "gx", split_axis=2, concat_axis=1, tiled=True)
    direct = jnp.einsum("zcxy,co->zoxy", lifted, mix_weight, preferred_element_type=jnp.float32)
    summed = direct + output_bias[None, :, None, None] + spectral.astype(jnp.float32)
    return jax.nn.gelu(summed, approximate=True).astype(jnp.bfloat16)


def solution(mesh):
    placed = (
        P(None, "ga", "gx", "gy"),
        P("ga", "gx", "gy"),
        P(),
        P(),
        P(),
        P("ga", "gy", None, "gx", None),
        P(),
    )
    return jax.shard_map(
        shards, mesh=mesh, in_specs=placed, out_specs=P("ga", None, "gx", "gy"), check_vma=False
    )
```

profile of v0, /device:TPU:4, one launch (start us, length us, event | category | flops | bytes accessed | tf_op | source)
XLA Modules:
  0.0 481.4 jit_solution(12632177929340682965)
XLA Ops:
  6.5 1.2 fusion.133
  7.7 3.7 collective-permute-start
  11.5 1.7 collective-permute-done
  13.1 4.4 collective-permute-done.1
  17.6 1.2 pad_maximum_fusion
  19.0 4.3 collective-permute-start.2
  23.3 9.0 %collective-permute-done.2 = f32[5,8,18,1]{3,2,1,0:T(8,128)S(1)} collective-permute-done((f32[5,8,18,1]{3,2,1,0:T(8,128)S(1)}, f32[5,8,18,1]{3,2,1,0:T(8,128)S(1)}, u32[]{:S(2)}, u32[]{:S(2)}) %collective-permute-start.2) | collective-permute-done | bytes 2912 | tf_op jit(solution)/shard_map/ppermute | solution.py:26
  32.4 5.8 %collective-permute-done.3 = f32[5,8,18,1]{3,2,1,0:T(8,128)S(1)} collective-permute-done((f32[5,8,18,1]{3,2,1,0:T(8,128)S(1)}, f32[5,8,18,1]{3,2,1,0:T(8,128)S(1)}, u32[]{:S(2)}, u32[]{:S(2)}) %collective-permute-start.3) | collective-permute-done | bytes 2912 | tf_op jit(solution)/shard_map/ppermute | solution.py:23
  40.8 1.2 multiply_add_fusion.2
  43.0 1.1 collective-permute-start.7
  44.2 2.1 collective-permute-done.6
  46.3 2.8 collective-permute-done.7
  49.6 2.0 collective-permute-start.9
  51.6 9.9 %collective-permute-done.8 = f32[5,8,18,1]{3,2,1,0:T(8,128)S(1)} collective-permute-done((f32[5,8,18,1]{3,2,1,0:T(8,128)S(1)}, f32[5,8,18,1]{3,2,1,0:T(8,128)S(1)}, u32[]{:S(2)}, u32[]{:S(2)}) %collective-permute-start.8) | collective-permute-done | bytes 2912 | tf_op jit(solution)/shard_map/ppermute | solution.py:26
  61.5 3.7 collective-permute-done.9
  67.8 1.2 multiply_add_fusion.1
  69.4 1.7 collective-permute-start.13
  71.2 2.1 collective-permute-done.12
  73.3 2.2 collective-permute-done.13
  76.0 2.2 collective-permute-start.15
  78.1 9.8 %collective-permute-done.14 = f32[5,8,18,1]{3,2,1,0:T(8,128)S(1)} collective-permute-done((f32[5,8,18,1]{3,2,1,0:T(8,128)S(1)}, f32[5,8,18,1]{3,2,1,0:T(8,128)S(1)}, u32[]{:S(2)}, u32[]{:S(2)}) %collective-permute-start.14) | collective-permute-done | bytes 2912 | tf_op jit(solution)/shard_map/ppermute | solution.py:26
  88.0 3.9 collective-permute-done.15
  94.5 1.2 multiply_add_fusion
  95.6 5.5 %copy.39 = f32[5,8,16,256]{1,3,2,0:T(8,128)} copy(f32[5,8,16,256]{3,2,1,0:T(8,128)S(1)} %multiply_add_fusion) | data formatting | bytes 1310720 | tf_op jit(solution)/shard_map/add | solution.py:56
  101.1 10.9 %fusion = f32[5,8,8,1,128,1]{1,5,4,3,2,0:T(1,128)S(1)} fusion(f32[5,8,8,2,128,2]{1,5,4,3,2,0:T(2,128)} %bitcast.176), kind=kLoop, calls=%fused_computation.2 | loop fusion | flops 163840 | bytes 819200 | tf_op jit(solution)/shard_map/mul | solution.py:62
  112.1 1.1 copy.40
  113.2 1.3 fusion.13
  116.4 3.5 all-to-all-start
  119.9 2.1 fusion.47
  122.3 8.2 %all-to-all-done = bf16[8,32,8,128]{3,2,0,1:T(8,128)(2,1)S(1)} async-done(((bf16[8,32,8,128]{3,2,0,1:T(8,128)(2,1)}), bf16[8,32,8,128]{3,2,0,1:T(8,128)(2,1)S(1)}, u32[]{:S(2)}, u32[]{:S(2)}) %all-to-all-start) | async-done | bytes 524320 | tf_op jit(solution)/shard_map/all_to_all | solution.py:189
  131.5 5.9 %all-to-all-start.1 = ((bf16[8,4,64,128]{3,2,1,0:T(8,128)(2,1)}), bf16[8,4,64,128]{3,2,1,0:T(8,128)(2,1)S(1)}, u32[]{:S(2)}, u32[]{:S(2)}) async-start(bf16[8,4,64,128]{3,2,1,0:T(8,128)(2,1)} %bitcast.173), calls=%async_computation.1 | async-start | bytes 1048576 | tf_op jit(solution)/shard_map/all_to_all | solution.py:188
  137.9 8.0 %all-to-all-done.1 = bf16[8,4,64,128]{3,2,1,0:T(8,128)(2,1)S(1)} async-done(((bf16[8,4,64,128]{3,2,1,0:T(8,128)(2,1)}), bf16[8,4,64,128]{3,2,1,0:T(8,128)(2,1)S(1)}, u32[]{:S(2)}, u32[]{:S(2)}) %all-to-all-start.1) | async-done | bytes 524320 | tf_op jit(solution)/shard_map/all_to_all | solution.py:188
  147.1 1.6 convolution_bitcast_fusion.2
  151.8 134.7 %all-reduce.3.cloned.1.call-done = bf16[16,4,4,4,128]{4,3,2,1,0:T(4,128)(2,1)} async-done(((bf16[16,4,4,4,128]{4,3,2,1,0:T(4,128)(2,1)}), bf16[16,4,4,4,128]{4,3,2,1,0:T(4,128)(2,1)}) %all-reduce.3.cloned.1.call-update) | async-done | bytes 262160
  286.6 1.3 dynamic-slice_convert_fusion
  287.9 28.9 %all-gather = f32[1,4,32,4,128]{4,3,2,1,0:T(4,128)S(1)} all-gather(f32[1,4,4,4,128]{4,3,2,1,0:T(4,128)S(1)} %dynamic-slice_convert_fusion), channel_id=2, replica_groups=mesh['gx'=8,'gy'=8,'ga'=2] {'gx'}, dimensions={2}, use_global_device_ids=true | all-gather | bytes 294912 | tf_op jit(solution)/shard_map/all_gather | solution.py:221
  317.1 1.4 multiply_reduce_fusion.3
  321.3 1.1 sine_multiply_fusion.1
  322.4 7.2 %reduce-scatter.2.cloned.1.call-done = f32[8,4,4,128]{3,0,2,1:T(8,128)} async-done(((f32[16,4,4,128]{3,0,2,1:T(8,128)}), f32[8,4,4,128]{3,0,2,1:T(8,128)}) %reduce-scatter.2.cloned.1.call-update) | async-done | bytes 65552 | tf_op jit(solution)/shard_map/reduce_scatter | solution.py:226
  329.7 1.8 fusion.24
  331.5 17.0 %copy.48 = f32[8,4,4,2,1024]{0,3,2,1,4:T(2,128)} copy(f32[8,4,4,2,1024]{4,0,3,2,1:T(8,128)S(1)} %fusion.24) | data formatting | bytes 2097152 | tf_op jit(solution)/shard_map/zomq,qpy->zompy/dot_general | solution.py:232
  348.6 28.9 %reshape.560 = f32[8,1,32768]{2,1,0:T(1,128)} reshape(f32[1024,4,4,2,8]{4,3,2,1,0:T(2,128)} %bitcast.174) | data formatting | bytes 2097152
  377.5 7.8 %all-to-all-start.2 = ((f32[8,1,32768]{2,1,0:T(1,128)}), f32[8,1,32768]{2,1,0:T(1,128)S(1)}, u32[]{:S(2)}, u32[]{:S(2)}) async-start(f32[8,1,32768]{2,1,0:T(1,128)} %reshape.560), calls=%async_computation.3 | async-start | bytes 2097152 | tf_op jit(solution)/shard_map/all_to_all | solution.py:238
  385.4 14.2 %all-to-all-done.2 = f32[8,1,32768]{2,1,0:T(1,128)S(1)} async-done(((f32[8,1,32768]{2,1,0:T(1,128)}), f32[8,1,32768]{2,1,0:T(1,128)S(1)}, u32[]{:S(2)}, u32[]{:S(2)}) %all-to-all-start.2) | async-done | bytes 1048608 | tf_op jit(solution)/shard_map/all_to_all | solution.py:238
  400.1 3.3 reduce.8
  403.4 32.2 %reshape.561 = f32[1024,4,4,2,8]{4,3,2,1,0:T(2,128)} reshape(f32[8,32768]{1,0:T(8,128)S(1)} %reduce.8) | data formatting | bytes 2097152
  435.6 20.6 %copy.49 = f32[8,4,4,2,8,128]{5,2,4,3,1,0:T(4,128)S(1)} copy(f32[8,4,4,2,8,128]{0,3,2,1,5,4:T(2,128)} %bitcast.175) | data formatting | bytes 2097152 | tf_op jit(solution)/shard_map/all_to_all | solution.py:238
  457.7 14.7 %all_to_all.60 = bf16[8,4,64,128]{3,1,0,2:T(4,128)(2,1)S(1)} all-to-all(bf16[8,4,64,128]{3,1,0,2:T(4,128)(2,1)S(1)} %copy.50), channel_id=1, replica_groups=mesh['gx'=8,'gy'=8,'ga'=2] {'gx'}, dimensions={2} | all-to-all | bytes 1048576 | tf_op jit(solution)/shard_map/all_to_all | solution.py:245
  (111 shorter events, 24.8 us)
Async XLA Ops:
  6.5 466.1 %copy-start = (bf16[32,32]{1,0:T(8,128)(2,1)S(1)}, bf16[32,32]{1,0:T(8,128)(2,1)}, u32[]{:S(2)}) copy-start(bf16[32,32]{1,0:T(8,128)(2,1)} %param.11) | copy-start | bytes 6148
  6.5 31.7 %copy-start.1 = (f32[5,8,16,256]{3,2,1,0:T(8,128)S(1)}, f32[5,8,16,256]{3,2,1,0:T(8,128)}, u32[]{:S(2)}) copy-start(f32[5,8,16,256]{3,2,1,0:T(8,128)} %param.7) | copy-start | bytes 1966084
  7.7 5.4 %collective-permute-start = (f32[5,8,1,256]{3,2,1,0:T(1,128)S(1)}, f32[5,8,1,256]{3,2,1,0:T(1,128)S(1)}, u32[]{:S(2)}, u32[]{:S(2)}) collective-permute-start(f32[5,8,1,256]{3,2,1,0:T(1,128)S(1)} %get-tuple-element.34), channel_id=1, source_target_pairs={{16,0},{32,16},{48,32},{64,48},{80,64},{96,80},{112,96},{0,112},{1... | collective-permute-start | bytes 122888 | tf_op jit(solution)/shard_map/ppermute | solution.py:26
  11.5 6.1 %collective-permute-start.1 = (f32[5,8,1,256]{3,2,1,0:T(1,128)S(1)}, f32[5,8,1,256]{3,2,1,0:T(1,128)S(1)}, u32[]{:S(2)}, u32[]{:S(2)}) collective-permute-start(f32[5,8,1,256]{3,2,1,0:T(1,128)S(1)} %get-tuple-element.33), channel_id=1, source_target_pairs={{0,16},{16,32},{32,48},{48,64},{64,80},{80,96},{96,112},{112,0},{1... | collective-permute-start | bytes 122888 | tf_op jit(solution)/shard_map/ppermute | solution.py:23
  19.0 13.4 %collective-permute-start.2 = (f32[5,8,18,1]{3,2,1,0:T(8,128)S(1)}, f32[5,8,18,1]{3,2,1,0:T(8,128)S(1)}, u32[]{:S(2)}, u32[]{:S(2)}) collective-permute-start(f32[5,8,18,1]{3,2,1,0:T(8,128)S(1)} %get-tuple-element.22), channel_id=1, source_target_pairs={{2,0},{4,2},{6,4},{8,6},{10,8},{12,10},{14,12},{0,14},{3,1},{5,3},... | collective-permute-start | bytes 8648 | tf_op jit(solution)/shard_map/ppermute | solution.py:26
  23.3 14.9 %collective-permute-start.3 = (f32[5,8,18,1]{3,2,1,0:T(8,128)S(1)}, f32[5,8,18,1]{3,2,1,0:T(8,128)S(1)}, u32[]{:S(2)}, u32[]{:S(2)}) collective-permute-start(f32[5,8,18,1]{3,2,1,0:T(8,128)S(1)} %get-tuple-element.21), channel_id=1, source_target_pairs={{0,2},{2,4},{4,6},{6,8},{8,10},{10,12},{12,14},{14,0},{1,3},{3,5},... | collective-permute-start | bytes 8648 | tf_op jit(solution)/shard_map/ppermute | solution.py:23
  38.5 1.5 collective-permute-start.4
  38.6 1.7 collective-permute-start.5
  39.8 1.0 copy-start.3
  42.1 4.2 collective-permute-start.6
  43.0 6.1 %collective-permute-start.7 = (f32[5,8,1,256]{3,2,1,0:T(1,128)S(1)}, f32[5,8,1,256]{3,2,1,0:T(1,128)S(1)}, u32[]{:S(2)}, u32[]{:S(2)}) collective-permute-start(f32[5,8,1,256]{3,2,1,0:T(1,128)S(1)} %get-tuple-element.31), channel_id=1, source_target_pairs={{0,16},{16,32},{32,48},{48,64},{64,80},{80,96},{96,112},{112,0},{1... | collective-permute-start | bytes 122888 | tf_op jit(solution)/shard_map/ppermute | solution.py:23
  49.5 12.0 %collective-permute-start.8 = (f32[5,8,18,1]{3,2,1,0:T(8,128)S(1)}, f32[5,8,18,1]{3,2,1,0:T(8,128)S(1)}, u32[]{:S(2)}, u32[]{:S(2)}) collective-permute-start(f32[5,8,18,1]{3,2,1,0:T(8,128)S(1)} %get-tuple-element.20), channel_id=1, source_target_pairs={{2,0},{4,2},{6,4},{8,6},{10,8},{12,10},{14,12},{0,14},{3,1},{5,3},... | collective-permute-start | bytes 8648 | tf_op jit(solution)/shard_map/ppermute | solution.py:26
  49.6 15.6 %collective-permute-start.9 = (f32[5,8,18,1]{3,2,1,0:T(8,128)S(1)}, f32[5,8,18,1]{3,2,1,0:T(8,128)S(1)}, u32[]{:S(2)}, u32[]{:S(2)}) collective-permute-start(f32[5,8,18,1]{3,2,1,0:T(8,128)S(1)} %get-tuple-element.19), channel_id=1, source_target_pairs={{0,2},{2,4},{4,6},{6,8},{8,10},{10,12},{12,14},{14,0},{1,3},{3,5},... | collective-permute-start | bytes 8648 | tf_op jit(solution)/shard_map/ppermute | solution.py:23
  65.5 1.5 collective-permute-start.10
  65.6 1.7 collective-permute-start.11
  69.1 4.2 collective-permute-start.12
  69.4 6.1 %collective-permute-start.13 = (f32[5,8,1,256]{3,2,1,0:T(1,128)S(1)}, f32[5,8,1,256]{3,2,1,0:T(1,128)S(1)}, u32[]{:S(2)}, u32[]{:S(2)}) collective-permute-start(f32[5,8,1,256]{3,2,1,0:T(1,128)S(1)} %get-tuple-element.29), channel_id=1, source_target_pairs={{0,16},{16,32},{32,48},{48,64},{64,80},{80,96},{96,112},{112,0},{1... | collective-permute-start | bytes 122888 | tf_op jit(solution)/shard_map/ppermute | solution.py:23
  75.9 12.1 %collective-permute-start.14 = (f32[5,8,18,1]{3,2,1,0:T(8,128)S(1)}, f32[5,8,18,1]{3,2,1,0:T(8,128)S(1)}, u32[]{:S(2)}, u32[]{:S(2)}) collective-permute-start(f32[5,8,18,1]{3,2,1,0:T(8,128)S(1)} %get-tuple-element.18), channel_id=1, source_target_pairs={{2,0},{4,2},{6,4},{8,6},{10,8},{12,10},{14,12},{0,14},{3,1},{5,3},... | collective-permute-start | bytes 8648 | tf_op jit(solution)/shard_map/ppermute | solution.py:26
  76.0 15.9 %collective-permute-start.15 = (f32[5,8,18,1]{3,2,1,0:T(8,128)S(1)}, f32[5,8,18,1]{3,2,1,0:T(8,128)S(1)}, u32[]{:S(2)}, u32[]{:S(2)}) collective-permute-start(f32[5,8,18,1]{3,2,1,0:T(8,128)S(1)} %get-tuple-element.17), channel_id=1, source_target_pairs={{0,2},{2,4},{4,6},{6,8},{8,10},{10,12},{12,14},{14,0},{1,3},{3,5},... | collective-permute-start | bytes 8648 | tf_op jit(solution)/shard_map/ppermute | solution.py:23
  92.1 1.5 collective-permute-start.16
  92.2 1.7 collective-permute-start.17
  112.0 1.2 copy-start.6
  112.1 1.2 copy-start.7
  114.6 0.8 copy-start.4
  116.4 14.2 %all-to-all-start = ((bf16[8,32,8,128]{3,2,0,1:T(8,128)(2,1)}), bf16[8,32,8,128]{3,2,0,1:T(8,128)(2,1)S(1)}, u32[]{:S(2)}, u32[]{:S(2)}) async-start(bf16[8,32,8,128]{3,2,0,1:T(8,128)(2,1)} %copy.42), calls=%async_computation | async-start | bytes 1048576 | tf_op jit(solution)/shard_map/all_to_all | solution.py:189
  131.5 14.4 %all-to-all-start.1 = ((bf16[8,4,64,128]{3,2,1,0:T(8,128)(2,1)}), bf16[8,4,64,128]{3,2,1,0:T(8,128)(2,1)S(1)}, u32[]{:S(2)}, u32[]{:S(2)}) async-start(bf16[8,4,64,128]{3,2,1,0:T(8,128)(2,1)} %bitcast.173), calls=%async_computation.1 | async-start | bytes 1048576 | tf_op jit(solution)/shard_map/all_to_all | solution.py:188
  137.4 149.2 %all-reduce.3.cloned.1.call-start = ((), (), s32[]{:S(2)}) async-start(), calls=%async_computation.6 | async-start | bytes 524288
  147.1 4.1 copy-start.9
  149.4 167.7 %copy-start.2 = (f32[4,4,32,4,128]{4,3,2,1,0:T(4,128)S(1)}, f32[4,4,32,4,128]{4,3,2,1,0:T(4,128)}, u32[]{:S(2)}) copy-start(f32[4,4,32,4,128]{4,3,2,1,0:T(4,128)} %param.12) | copy-start | bytes 3145732
  151.1 178.5 %reduce-scatter.2.cloned.1.call-start = ((), (), s32[]{:S(2)}) async-start(), calls=%async_computation.5 | async-start | bytes 196608 | tf_op jit(solution)/shard_map/reduce_scatter | solution.py:226
  377.5 22.1 %all-to-all-start.2 = ((f32[8,1,32768]{2,1,0:T(1,128)}), f32[8,1,32768]{2,1,0:T(1,128)S(1)}, u32[]{:S(2)}, u32[]{:S(2)}) async-start(f32[8,1,32768]{2,1,0:T(1,128)} %reshape.560), calls=%async_computation.3 | async-start | bytes 2097152 | tf_op jit(solution)/shard_map/all_to_all | solution.py:238
  456.2 16.5 %copy-start.5 = (bf16[8,32,8,128]{3,1,2,0:T(8,128)(2,1)S(1)}, bf16[8,32,8,128]{3,1,2,0:T(8,128)(2,1)}, u32[]{:S(2)}) copy-start(bf16[8,32,8,128]{3,1,2,0:T(8,128)(2,1)} %copy-done.4) | copy-start | bytes 1572868
  456.2 16.5 %copy-start.8 = (f32[32]{0:T(128)S(1)}, f32[32]{0:T(128)}, u32[]{:S(2)}) copy-start(f32[32]{0:T(128)} %param.13) | copy-start | bytes 388
Sparse Core Ops, SparseCore 0:
  151.2 135.2 all-reduce.2
  321.4 8.2 reduce-scatter.1
where the time goes:
time: 491 us; the launch traced here: 481 us
  waiting for transfers between devices  232 us (47%)
  local copies, waits for them, and re-layouts  115 us (23%)
  blocking collectives  43.6 us (9%)
  starting transfers between devices  35.7 us (7%)
  other arithmetic  32.6 us (7%)
  between operations  14.2 us (3%)
  matrix products  8.66 us (2%)
    unnamed x3, waiting for transfers between devices  135 us
    unnamed x35, local copies, waits for them, and re-layouts  63 us
    ppermute x9, waiting for transfers between devices, padded_2(): lax.ppermute(lax.slice_in_dim(block, 0, width, axis=dim), axis, backward)  35.4 us
    all_gather x1, blocking collectives, shards(): lax.all_gather(coeffs, 'gx', axis=1, tiled=True)  28.9 us
    ppermute x9, waiting for transfers between devices, padded_2(): lax.ppermute(lax.slice_in_dim(block, block.shape[dim] - width, None, axis...  23.7 us
    all_to_all x2, local copies, waits for them, and re-layouts, shards(): lax.all_to_all(back_north, 'gy', split_axis=4, concat_axis=2, tiled=True)  21.1 us
    dot_general x1, local copies, waits for them, and re-layouts, shards(): jnp.einsum('zomq,qpy->zompy', back_depth, inverse_north_table(north_point...  17 us
    all_to_all x1, blocking collectives, shards(): lax.all_to_all(spectral, 'gx', split_axis=2, concat_axis=1, tiled=True)  14.7 us
  transfers between devices with their start and end apart: 23, of which 23 were waited for; matrix products, arithmetic and copies ran while one was open for 1% of the time, Pallas kernels for 0%

commit v1 on v0

--- a/solution.py
+++ b/solution.py
@@ -218,7 +218,12 @@
         scatter_dimension=0,
         tiled=True,
     ).astype(jnp.float32)[0]
-    mixed_modes = mix_channels(lax.all_gather(coeffs, "gx", axis=1, tiled=True), spectral_weight)
+    mixed_modes = mix_channels(
+        jnp.concatenate(
+            lax.all_to_all(jnp.stack([coeffs] * lax.axis_size("gx")), "gx", 0, 0), axis=1
+        ),
+        spectral_weight,
+    )
     own_frequencies = lax.axis_index("ga") * coeffs.shape[0] + jnp.arange(
         coeffs.shape[0], dtype=jnp.int32
     )

time: 491 us -> 475 us (0.967)
  blocking collectives: 43.6 us -> 14.7 us
  waiting for transfers between devices: 232 us -> 239 us
    all_gather x1 -> x0, blocking collectives: 28.9 us -> none  [shards(): lax.all_gather(coeffs, 'gx', axis=1, tiled=True)]
    all_to_all x0 -> x1, waiting for transfers between devices: none -> 7.22 us  [shards(): lax.all_to_all(jnp.stack([coeffs] * lax.axis_size('gx')), 'gx', 0, 0)]
    unnamed x35 -> x33, local copies, waits for them, and re-layouts: 63 us -> 62.9 us
  transfers between devices with their start and end apart: 23 -> 24, of which waited for: 23 -> 24; matrix products, arithmetic and copies ran while one was open for 1% -> 1% of each run, Pallas kernels for 0% -> 0%
where the time goes in v1:
time: 475 us; the launch traced here: 466 us
  waiting for transfers between devices  239 us (50%)
  local copies, waits for them, and re-layouts  116 us (24%)
  starting transfers between devices  40.6 us (9%)
  other arithmetic  32.7 us (7%)
  blocking collectives  14.7 us (3%)
  between operations  14.3 us (3%)
  matrix products  8.68 us (2%)
    unnamed x3, waiting for transfers between devices  135 us
    unnamed x33, local copies, waits for them, and re-layouts  62.9 us
    ppermute x9, waiting for transfers between devices, padded_2(): lax.ppermute(lax.slice_in_dim(block, 0, width, axis=dim), axis, backward)  35.4 us
    ppermute x9, waiting for transfers between devices, padded_2(): lax.ppermute(lax.slice_in_dim(block, block.shape[dim] - width, None, axis...  23.7 us
    all_to_all x2, local copies, waits for them, and re-layouts, shards(): lax.all_to_all(back_north, 'gy', split_axis=4, concat_axis=2, tiled=True)  21.1 us
    dot_general x1, local copies, waits for them, and re-layouts, shards(): jnp.einsum('zomq,qpy->zompy', back_depth, inverse_north_table(north_point...  17 us
    all_to_all x1, blocking collectives, shards(): lax.all_to_all(spectral, 'gx', split_axis=2, concat_axis=1, tiled=True)  14.7 us
    all_to_all x1, waiting for transfers between devices, shards(): lax.all_to_all(back_north, 'gy', split_axis=4, concat_axis=2, tiled=True)  14.2 us
  transfers between devices with their start and end apart: 24, of which 24 were waited for; matrix products, arithmetic and copies ran while one was open for 1% of the time, Pallas kernels for 0%

profile of v1, /device:TPU:4, one launch (start us, length us, event | category | flops | bytes accessed | tf_op | source)
XLA Modules:
  0.0 465.8 jit_solution(4253091089648335298)
XLA Ops:
  6.5 1.2 fusion.133
  7.7 3.7 collective-permute-start
  11.5 1.7 collective-permute-done
  13.1 4.4 collective-permute-done.1
  17.6 1.2 pad_maximum_fusion
  19.0 4.3 collective-permute-start.2
  23.3 9.0 %collective-permute-done.2 = f32[5,8,18,1]{3,2,1,0:T(8,128)S(1)} collective-permute-done((f32[5,8,18,1]{3,2,1,0:T(8,128)S(1)}, f32[5,8,18,1]{3,2,1,0:T(8,128)S(1)}, u32[]{:S(2)}, u32[]{:S(2)}) %collective-permute-start.2) | collective-permute-done | bytes 2912 | tf_op jit(solution)/shard_map/ppermute | solution.py:26
  32.4 5.8 %collective-permute-done.3 = f32[5,8,18,1]{3,2,1,0:T(8,128)S(1)} collective-permute-done((f32[5,8,18,1]{3,2,1,0:T(8,128)S(1)}, f32[5,8,18,1]{3,2,1,0:T(8,128)S(1)}, u32[]{:S(2)}, u32[]{:S(2)}) %collective-permute-start.3) | collective-permute-done | bytes 2912 | tf_op jit(solution)/shard_map/ppermute | solution.py:23
  40.8 1.2 multiply_add_fusion.2
  43.0 1.1 collective-permute-start.7
  44.2 2.1 collective-permute-done.6
  46.3 2.8 collective-permute-done.7
  49.6 2.0 collective-permute-start.9
  51.6 9.9 %collective-permute-done.8 = f32[5,8,18,1]{3,2,1,0:T(8,128)S(1)} collective-permute-done((f32[5,8,18,1]{3,2,1,0:T(8,128)S(1)}, f32[5,8,18,1]{3,2,1,0:T(8,128)S(1)}, u32[]{:S(2)}, u32[]{:S(2)}) %collective-permute-start.8) | collective-permute-done | bytes 2912 | tf_op jit(solution)/shard_map/ppermute | solution.py:26
  61.5 3.7 collective-permute-done.9
  67.8 1.2 multiply_add_fusion.1
  69.4 1.7 collective-permute-start.13
  71.2 2.1 collective-permute-done.12
  73.3 2.2 collective-permute-done.13
  76.0 2.2 collective-permute-start.15
  78.1 9.8 %collective-permute-done.14 = f32[5,8,18,1]{3,2,1,0:T(8,128)S(1)} collective-permute-done((f32[5,8,18,1]{3,2,1,0:T(8,128)S(1)}, f32[5,8,18,1]{3,2,1,0:T(8,128)S(1)}, u32[]{:S(2)}, u32[]{:S(2)}) %collective-permute-start.14) | collective-permute-done | bytes 2912 | tf_op jit(solution)/shard_map/ppermute | solution.py:26
  88.0 3.9 collective-permute-done.15
  94.5 1.2 multiply_add_fusion
  95.6 5.4 %copy.44 = f32[5,8,16,256]{1,3,2,0:T(8,128)} copy(f32[5,8,16,256]{3,2,1,0:T(8,128)S(1)} %multiply_add_fusion) | data formatting | bytes 1310720 | tf_op jit(solution)/shard_map/add | solution.py:56
  101.1 10.9 %fusion = f32[5,8,8,1,128,1]{1,5,4,3,2,0:T(1,128)S(1)} fusion(f32[5,8,8,2,128,2]{1,5,4,3,2,0:T(2,128)} %bitcast.180), kind=kLoop, calls=%fused_computation.2 | loop fusion | flops 163840 | bytes 819200 | tf_op jit(solution)/shard_map/mul | solution.py:62
  112.0 1.1 copy.45
  113.1 1.3 fusion.13
  116.3 3.5 all-to-all-start
  119.8 2.1 fusion.47
  122.2 8.2 %all-to-all-done = bf16[8,32,8,128]{3,2,0,1:T(8,128)(2,1)S(1)} async-done(((bf16[8,32,8,128]{3,2,0,1:T(8,128)(2,1)}), bf16[8,32,8,128]{3,2,0,1:T(8,128)(2,1)S(1)}, u32[]{:S(2)}, u32[]{:S(2)}) %all-to-all-start) | async-done | bytes 524320 | tf_op jit(solution)/shard_map/all_to_all | solution.py:189
  131.4 5.9 %all-to-all-start.1 = ((bf16[8,4,64,128]{3,2,1,0:T(8,128)(2,1)}), bf16[8,4,64,128]{3,2,1,0:T(8,128)(2,1)S(1)}, u32[]{:S(2)}, u32[]{:S(2)}) async-start(bf16[8,4,64,128]{3,2,1,0:T(8,128)(2,1)} %bitcast.177), calls=%async_computation.1 | async-start | bytes 1048576 | tf_op jit(solution)/shard_map/all_to_all | solution.py:188
  137.8 8.0 %all-to-all-done.1 = bf16[8,4,64,128]{3,2,1,0:T(8,128)(2,1)S(1)} async-done(((bf16[8,4,64,128]{3,2,1,0:T(8,128)(2,1)}), bf16[8,4,64,128]{3,2,1,0:T(8,128)(2,1)S(1)}, u32[]{:S(2)}, u32[]{:S(2)}) %all-to-all-start.1) | async-done | bytes 524320 | tf_op jit(solution)/shard_map/all_to_all | solution.py:188
  147.0 1.6 convolution_bitcast_fusion.2
  151.8 135.0 %all-reduce.3.cloned.1.call-done = bf16[16,4,4,4,128]{4,2,3,1,0:T(4,128)(2,1)} async-done(((bf16[16,4,4,4,128]{4,2,3,1,0:T(4,128)(2,1)}), bf16[16,4,4,4,128]{4,2,3,1,0:T(4,128)(2,1)}) %all-reduce.3.cloned.1.call-update) | async-done | bytes 262160
  286.8 1.4 bitcast_convert_fusion
  288.9 4.9 %all-to-all-start.2 = ((f32[8,4,4,4,128]{4,2,3,1,0:T(4,128)}), f32[8,4,4,4,128]{4,2,3,1,0:T(4,128)S(1)}, u32[]{:S(2)}, u32[]{:S(2)}) async-start(f32[8,4,4,4,128]{4,2,3,1,0:T(4,128)} %stack.64), calls=%async_computation.2 | async-start | bytes 524288 | tf_op jit(solution)/shard_map/all_to_all | solution.py:223
  293.9 7.2 %all-to-all-done.2 = f32[8,4,4,4,128]{4,2,3,1,0:T(4,128)S(1)} async-done(((f32[8,4,4,4,128]{4,2,3,1,0:T(4,128)}), f32[8,4,4,4,128]{4,2,3,1,0:T(4,128)S(1)}, u32[]{:S(2)}, u32[]{:S(2)}) %all-to-all-start.2) | async-done | bytes 262176 | tf_op jit(solution)/shard_map/all_to_all | solution.py:223
  301.3 1.4 multiply_reduce_fusion.3
  306.6 7.5 %reduce-scatter.2.cloned.1.call-done = f32[8,4,4,128]{3,0,2,1:T(8,128)} async-done(((f32[16,4,4,128]{3,0,2,1:T(8,128)}), f32[8,4,4,128]{3,0,2,1:T(8,128)}) %reduce-scatter.2.cloned.1.call-update) | async-done | bytes 65552 | tf_op jit(solution)/shard_map/reduce_scatter | solution.py:231
  314.1 1.8 fusion.24
  316.0 17.0 %copy.56 = f32[8,4,4,2,1024]{0,3,2,1,4:T(2,128)} copy(f32[8,4,4,2,1024]{4,0,3,2,1:T(8,128)S(1)} %fusion.24) | data formatting | bytes 2097152 | tf_op jit(solution)/shard_map/zomq,qpy->zompy/dot_general | solution.py:237
  333.0 29.0 %reshape.569 = f32[8,1,32768]{2,1,0:T(1,128)} reshape(f32[1024,4,4,2,8]{4,3,2,1,0:T(2,128)} %bitcast.178) | data formatting | bytes 2097152
  362.0 7.8 %all-to-all-start.3 = ((f32[8,1,32768]{2,1,0:T(1,128)}), f32[8,1,32768]{2,1,0:T(1,128)S(1)}, u32[]{:S(2)}, u32[]{:S(2)}) async-start(f32[8,1,32768]{2,1,0:T(1,128)} %reshape.569), calls=%async_computation.4 | async-start | bytes 2097152 | tf_op jit(solution)/shard_map/all_to_all | solution.py:243
  369.9 14.2 %all-to-all-done.3 = f32[8,1,32768]{2,1,0:T(1,128)S(1)} async-done(((f32[8,1,32768]{2,1,0:T(1,128)}), f32[8,1,32768]{2,1,0:T(1,128)S(1)}, u32[]{:S(2)}, u32[]{:S(2)}) %all-to-all-start.3) | async-done | bytes 1048608 | tf_op jit(solution)/shard_map/all_to_all | solution.py:243
  384.6 3.3 reduce.8
  387.8 32.2 %reshape.570 = f32[1024,4,4,2,8]{4,3,2,1,0:T(2,128)} reshape(f32[8,32768]{1,0:T(8,128)S(1)} %reduce.8) | data formatting | bytes 2097152
  420.1 20.6 %copy.57 = f32[8,4,4,2,8,128]{5,2,4,3,1,0:T(4,128)S(1)} copy(f32[8,4,4,2,8,128]{0,3,2,1,5,4:T(2,128)} %bitcast.179) | data formatting | bytes 2097152 | tf_op jit(solution)/shard_map/all_to_all | solution.py:243
  442.1 14.7 %all_to_all.65 = bf16[8,4,64,128]{3,1,0,2:T(4,128)(2,1)S(1)} all-to-all(bf16[8,4,64,128]{3,1,0,2:T(4,128)(2,1)S(1)} %copy.58), channel_id=1, replica_groups=mesh['gx'=8,'gy'=8,'ga'=2] {'gx'}, dimensions={2} | all-to-all | bytes 1048576 | tf_op jit(solution)/shard_map/all_to_all | solution.py:250
  (114 shorter events, 26.7 us)
Async XLA Ops:
  6.5 450.6 %copy-start = (bf16[32,32]{1,0:T(8,128)(2,1)S(1)}, bf16[32,32]{1,0:T(8,128)(2,1)}, u32[]{:S(2)}) copy-start(bf16[32,32]{1,0:T(8,128)(2,1)} %param.11) | copy-start | bytes 6148
  6.5 31.7 %copy-start.1 = (f32[5,8,16,256]{3,2,1,0:T(8,128)S(1)}, f32[5,8,16,256]{3,2,1,0:T(8,128)}, u32[]{:S(2)}) copy-start(f32[5,8,16,256]{3,2,1,0:T(8,128)} %param.7) | copy-start | bytes 1966084
  7.7 5.4 %collective-permute-start = (f32[5,8,1,256]{3,2,1,0:T(1,128)S(1)}, f32[5,8,1,256]{3,2,1,0:T(1,128)S(1)}, u32[]{:S(2)}, u32[]{:S(2)}) collective-permute-start(f32[5,8,1,256]{3,2,1,0:T(1,128)S(1)} %get-tuple-element.34), channel_id=1, source_target_pairs={{16,0},{32,16},{48,32},{64,48},{80,64},{96,80},{112,96},{0,112},{1... | collective-permute-start | bytes 122888 | tf_op jit(solution)/shard_map/ppermute | solution.py:26
  11.5 6.1 %collective-permute-start.1 = (f32[5,8,1,256]{3,2,1,0:T(1,128)S(1)}, f32[5,8,1,256]{3,2,1,0:T(1,128)S(1)}, u32[]{:S(2)}, u32[]{:S(2)}) collective-permute-start(f32[5,8,1,256]{3,2,1,0:T(1,128)S(1)} %get-tuple-element.33), channel_id=1, source_target_pairs={{0,16},{16,32},{32,48},{48,64},{64,80},{80,96},{96,112},{112,0},{1... | collective-permute-start | bytes 122888 | tf_op jit(solution)/shard_map/ppermute | solution.py:23
  19.0 13.4 %collective-permute-start.2 = (f32[5,8,18,1]{3,2,1,0:T(8,128)S(1)}, f32[5,8,18,1]{3,2,1,0:T(8,128)S(1)}, u32[]{:S(2)}, u32[]{:S(2)}) collective-permute-start(f32[5,8,18,1]{3,2,1,0:T(8,128)S(1)} %get-tuple-element.22), channel_id=1, source_target_pairs={{2,0},{4,2},{6,4},{8,6},{10,8},{12,10},{14,12},{0,14},{3,1},{5,3},... | collective-permute-start | bytes 8648 | tf_op jit(solution)/shard_map/ppermute | solution.py:26
  23.3 14.9 %collective-permute-start.3 = (f32[5,8,18,1]{3,2,1,0:T(8,128)S(1)}, f32[5,8,18,1]{3,2,1,0:T(8,128)S(1)}, u32[]{:S(2)}, u32[]{:S(2)}) collective-permute-start(f32[5,8,18,1]{3,2,1,0:T(8,128)S(1)} %get-tuple-element.21), channel_id=1, source_target_pairs={{0,2},{2,4},{4,6},{6,8},{8,10},{10,12},{12,14},{14,0},{1,3},{3,5},... | collective-permute-start | bytes 8648 | tf_op jit(solution)/shard_map/ppermute | solution.py:23
  38.5 1.5 collective-permute-start.4
  38.6 1.7 collective-permute-start.5
  39.8 1.0 copy-start.3
  42.1 4.2 collective-permute-start.6
  43.0 6.1 %collective-permute-start.7 = (f32[5,8,1,256]{3,2,1,0:T(1,128)S(1)}, f32[5,8,1,256]{3,2,1,0:T(1,128)S(1)}, u32[]{:S(2)}, u32[]{:S(2)}) collective-permute-start(f32[5,8,1,256]{3,2,1,0:T(1,128)S(1)} %get-tuple-element.31), channel_id=1, source_target_pairs={{0,16},{16,32},{32,48},{48,64},{64,80},{80,96},{96,112},{112,0},{1... | collective-permute-start | bytes 122888 | tf_op jit(solution)/shard_map/ppermute | solution.py:23
  49.5 12.0 %collective-permute-start.8 = (f32[5,8,18,1]{3,2,1,0:T(8,128)S(1)}, f32[5,8,18,1]{3,2,1,0:T(8,128)S(1)}, u32[]{:S(2)}, u32[]{:S(2)}) collective-permute-start(f32[5,8,18,1]{3,2,1,0:T(8,128)S(1)} %get-tuple-element.20), channel_id=1, source_target_pairs={{2,0},{4,2},{6,4},{8,6},{10,8},{12,10},{14,12},{0,14},{3,1},{5,3},... | collective-permute-start | bytes 8648 | tf_op jit(solution)/shard_map/ppermute | solution.py:26
  49.6 15.6 %collective-permute-start.9 = (f32[5,8,18,1]{3,2,1,0:T(8,128)S(1)}, f32[5,8,18,1]{3,2,1,0:T(8,128)S(1)}, u32[]{:S(2)}, u32[]{:S(2)}) collective-permute-start(f32[5,8,18,1]{3,2,1,0:T(8,128)S(1)} %get-tuple-element.19), channel_id=1, source_target_pairs={{0,2},{2,4},{4,6},{6,8},{8,10},{10,12},{12,14},{14,0},{1,3},{3,5},... | collective-permute-start | bytes 8648 | tf_op jit(solution)/shard_map/ppermute | solution.py:23
  65.5 1.5 collective-permute-start.10
  65.6 1.7 collective-permute-start.11
  69.1 4.2 collective-permute-start.12
  69.4 6.1 %collective-permute-start.13 = (f32[5,8,1,256]{3,2,1,0:T(1,128)S(1)}, f32[5,8,1,256]{3,2,1,0:T(1,128)S(1)}, u32[]{:S(2)}, u32[]{:S(2)}) collective-permute-start(f32[5,8,1,256]{3,2,1,0:T(1,128)S(1)} %get-tuple-element.29), channel_id=1, source_target_pairs={{0,16},{16,32},{32,48},{48,64},{64,80},{80,96},{96,112},{112,0},{1... | collective-permute-start | bytes 122888 | tf_op jit(solution)/shard_map/ppermute | solution.py:23
  75.9 12.1 %collective-permute-start.14 = (f32[5,8,18,1]{3,2,1,0:T(8,128)S(1)}, f32[5,8,18,1]{3,2,1,0:T(8,128)S(1)}, u32[]{:S(2)}, u32[]{:S(2)}) collective-permute-start(f32[5,8,18,1]{3,2,1,0:T(8,128)S(1)} %get-tuple-element.18), channel_id=1, source_target_pairs={{2,0},{4,2},{6,4},{8,6},{10,8},{12,10},{14,12},{0,14},{3,1},{5,3},... | collective-permute-start | bytes 8648 | tf_op jit(solution)/shard_map/ppermute | solution.py:26
  76.0 15.9 %collective-permute-start.15 = (f32[5,8,18,1]{3,2,1,0:T(8,128)S(1)}, f32[5,8,18,1]{3,2,1,0:T(8,128)S(1)}, u32[]{:S(2)}, u32[]{:S(2)}) collective-permute-start(f32[5,8,18,1]{3,2,1,0:T(8,128)S(1)} %get-tuple-element.17), channel_id=1, source_target_pairs={{0,2},{2,4},{4,6},{6,8},{8,10},{10,12},{12,14},{14,0},{1,3},{3,5},... | collective-permute-start | bytes 8648 | tf_op jit(solution)/shard_map/ppermute | solution.py:23
  92.1 1.5 collective-permute-start.16
  92.2 1.7 collective-permute-start.17
  111.9 1.2 copy-start.6
  112.0 1.2 copy-start.7
  114.5 0.8 copy-start.4
  116.3 14.2 %all-to-all-start = ((bf16[8,32,8,128]{3,2,0,1:T(8,128)(2,1)}), bf16[8,32,8,128]{3,2,0,1:T(8,128)(2,1)S(1)}, u32[]{:S(2)}, u32[]{:S(2)}) async-start(bf16[8,32,8,128]{3,2,0,1:T(8,128)(2,1)} %copy.47), calls=%async_computation | async-start | bytes 1048576 | tf_op jit(solution)/shard_map/all_to_all | solution.py:189
  131.4 14.4 %all-to-all-start.1 = ((bf16[8,4,64,128]{3,2,1,0:T(8,128)(2,1)}), bf16[8,4,64,128]{3,2,1,0:T(8,128)(2,1)S(1)}, u32[]{:S(2)}, u32[]{:S(2)}) async-start(bf16[8,4,64,128]{3,2,1,0:T(8,128)(2,1)} %bitcast.177), calls=%async_computation.1 | async-start | bytes 1048576 | tf_op jit(solution)/shard_map/all_to_all | solution.py:188
  137.3 149.4 %all-reduce.3.cloned.1.call-start = ((), (), s32[]{:S(2)}) async-start(), calls=%async_computation.7 | async-start | bytes 524288
  147.0 4.1 copy-start.9
  149.4 151.9 %copy-start.2 = (f32[4,4,32,4,128]{4,3,2,1,0:T(4,128)S(1)}, f32[4,4,32,4,128]{4,3,2,1,0:T(4,128)}, u32[]{:S(2)}) copy-start(f32[4,4,32,4,128]{4,3,2,1,0:T(4,128)} %param.12) | copy-start | bytes 3145732
  288.9 12.2 %all-to-all-start.2 = ((f32[8,4,4,4,128]{4,2,3,1,0:T(4,128)}), f32[8,4,4,4,128]{4,2,3,1,0:T(4,128)S(1)}, u32[]{:S(2)}, u32[]{:S(2)}) async-start(f32[8,4,4,4,128]{4,2,3,1,0:T(4,128)} %stack.64), calls=%async_computation.2 | async-start | bytes 524288 | tf_op jit(solution)/shard_map/all_to_all | solution.py:223
  293.8 20.3 %reduce-scatter.2.cloned.1.call-start = ((), (), s32[]{:S(2)}) async-start(), calls=%async_computation.6 | async-start | bytes 196608 | tf_op jit(solution)/shard_map/reduce_scatter | solution.py:231
  362.0 22.1 %all-to-all-start.3 = ((f32[8,1,32768]{2,1,0:T(1,128)}), f32[8,1,32768]{2,1,0:T(1,128)S(1)}, u32[]{:S(2)}, u32[]{:S(2)}) async-start(f32[8,1,32768]{2,1,0:T(1,128)} %reshape.569), calls=%async_computation.4 | async-start | bytes 2097152 | tf_op jit(solution)/shard_map/all_to_all | solution.py:243
  440.6 16.5 %copy-start.5 = (bf16[8,32,8,128]{3,1,2,0:T(8,128)(2,1)S(1)}, bf16[8,32,8,128]{3,1,2,0:T(8,128)(2,1)}, u32[]{:S(2)}) copy-start(bf16[8,32,8,128]{3,1,2,0:T(8,128)(2,1)} %copy-done.4) | copy-start | bytes 1572868
  440.7 16.5 %copy-start.8 = (f32[32]{0:T(128)S(1)}, f32[32]{0:T(128)}, u32[]{:S(2)}) copy-start(f32[32]{0:T(128)} %param.13) | copy-start | bytes 388
Sparse Core Ops, SparseCore 0:
  151.2 135.4 all-reduce.2
  305.6 8.4 reduce-scatter.1
